TPU v7x, 32 devices: a whole 2x2x4 slice. The times are simulated.
32 devices in a mesh: dp: 4 (over x, core), ens: 8 (over z, y).
Axes of the slice: x: 2, y: 2, z: 4, core: 2. Of those that a mesh axis runs over, the one named last changes fastest.
Arguments:
- embed: bfloat16 [4, 128, 128, 256], P('dp', 'ens'), may hold values from -6 to 6
- counts: int32 [4, 128], P('dp', 'ens'), may hold values from 4 to 128, as said below
- member: int32 [4, 128], P('dp', 'ens'), may hold values from 0 to 3, as said below
- bins: int32 [4, 128, 128, 128], P('dp', 'ens'), may hold values from 0 to 7
- masses: float32 [4, 4], P('dp'), may hold values from -1.5 to 1.5
- gain_attn: float32 [1, 256], replicated, may hold values from 0.25 to 1.75
- w_qkv: bfloat16 [1, 256, 768], replicated, may hold values from -0.375 to 0.375
- w_out: bfloat16 [1, 256, 256], replicated, may hold values from -0.375 to 0.375
- pair_table: float32 [1, 8, 8], replicated, may hold values from -4 to 4
- gain_ffn: float32 [1, 256], replicated, may hold values from 0.25 to 1.75
- w_up: bfloat16 [1, 256, 1024], replicated, may hold values from -0.375 to 0.375
- w_down: bfloat16 [1, 1024, 256], replicated, may hold values from -0.1875 to 0.1875
- w_phi: bfloat16 [256, 256], replicated, may hold values from -0.375 to 0.375
- w_mean: float32 [256], replicated, may hold values from -0.375 to 0.375
- w_scale: float32 [256], replicated, may hold values from -0.375 to 0.375
Outputs:
- neg_loglik: float32 [4, 4], P('dp')
- grad_gain_attn: float32 [1, 256], replicated
- grad_w_qkv: float32 [1, 256, 768], replicated
- grad_w_out: float32 [1, 256, 256], replicated
- grad_pair_table: float32 [1, 8, 8], replicated
- grad_gain_ffn: float32 [1, 256], replicated
- grad_w_up: float32 [1, 256, 1024], replicated
- grad_w_down: float32 [1, 1024, 256], replicated
- grad_w_phi: float32 [256, 256], replicated
- grad_w_mean: float32 [256], replicated
- grad_w_scale: float32 [256], replicated
Inputs may be any that keep to these rules, and one draw needn't show every extreme that they name: `counts`: every run of 16 consecutive jets of a group holds a jet with 128 constituents. `member`: every run of 16 consecutive jets of a group holds at least one jet of each ensemble.
All inputs are finite; a program needn't handle non-finite values.
Results may differ from a plain program's by a relative error of at most 0.028.
Values sent between devices are 32-bit elements; how exact they have to be, the bound alone decides.
A program may use at most 128 MiB of HBM per device.

v0:
```python
import functools
import math

import jax
import jax.numpy as jnp
from jax import lax
from jax.experimental import pallas as pl
from jax.experimental.pallas import tpu as pltpu
from jax.sharding import PartitionSpec as P

F32 = jnp.float32
BF16 = jnp.bfloat16
TOGETHER = 2
GELU_A = math.sqrt(2.0 / math.pi)
GELU_B = 0.044715


def dot(a, b, ca=1, cb=0):
    return lax.dot_general(a, b, (((ca,), (cb,)), ((), ())), preferred_element_type=F32)


def center(rows):
    average = jnp.mean(rows, axis=-1, keepdims=True)
    centred = rows - average
    variance = jnp.mean(centred * centred, axis=-1, keepdims=True)
    inverse = lax.rsqrt(variance + 1e-05)
    return centred * inverse, inverse


def center_back(d_hat, hat, inverse):
    first = jnp.mean(d_hat, axis=-1, keepdims=True)
    second = jnp.mean(d_hat * hat, axis=-1, keepdims=True)
    return inverse * (d_hat - first - hat * second)


def gelu_tanh(u):
    return jnp.tanh(GELU_A * (u + GELU_B * (u * u * u)))


def head_lanes(slots, width, heads):
    head_of = lax.broadcasted_iota(jnp.int32, (slots, width), 1) // (width // heads)
    return [head_of == h for h in range(heads)]


def spread(rows, lanes):
    return jnp.concatenate([rows * m.astype(F32).astype(BF16) for m in lanes], axis=0)


def collect(stacked, lanes, slots):
    out = stacked[0:slots]
    for h in range(1, len(lanes)):
        out = jnp.where(lanes[h], stacked[h * slots : (h + 1) * slots], out)
    return out


def forward_kernel(
    counts, table, x_ref, bins_ref, g1, w_qkv, w_out, g2, w_up, w_down,
    proj_o, att_o, ctx_o, mid_o, pooled_o,
):
    step = pl.program_id(0)
    slots = bins_ref.shape[1]
    width = x_ref.shape[1]
    heads = table.shape[1]
    scale = 1.0 / math.sqrt(width // heads)
    lanes = head_lanes(slots, width, heads)
    x = x_ref[...].astype(F32)
    hat, _ = center(x)
    normed = (hat * g1[...]).astype(BF16)
    proj = dot(normed, w_qkv[...]).astype(BF16)
    proj_o[...] = proj
    for j in range(TOGETHER):
        length = counts[step * TOGETHER + j]
        rows = slice(j * slots, (j + 1) * slots)
        queries = spread(proj[rows, 0:width], lanes)
        keys = proj[rows, width : 2 * width]
        values = proj[rows, 2 * width : 3 * width]
        raw = dot(keys, queries, 1, 1)
        levels = bins_ref[j].T
        bit0 = (levels & 1) == 1
        bit1 = (levels & 2) == 2
        bit2 = (levels & 4) == 4
        live = lax.broadcasted_iota(jnp.int32, (slots, slots), 0) < length
        pieces = []
        for h in range(heads):
            pair = [jnp.where(bit0, table[2 * i + 1, h], table[2 * i, h]) for i in range(4)]
            low = jnp.where(bit1, pair[1], pair[0])
            high = jnp.where(bit1, pair[3], pair[2])
            bias = jnp.where(bit2, high, low)
            score = raw[:, h * slots : (h + 1) * slots] * scale + bias
            score = jnp.where(live, score, -1e30)
            top = jnp.max(score, axis=0, keepdims=True)
            power = jnp.exp(score - top)
            total = jnp.sum(power, axis=0, keepdims=True)
            pieces.append((power * (1.0 / total)).astype(BF16))
        attend = jnp.concatenate(pieces, axis=1)
        att_o[j] = attend
        context = collect(dot(attend, values, 0, 0), lanes, slots)
        ctx_o[rows, :] = context.astype(BF16)
    middle = x + dot(ctx_o[...], w_out[...])
    mid_o[...] = middle
    hat, _ = center(middle)
    normed = (hat * g2[...]).astype(BF16)
    u = dot(normed, w_up[...])
    hidden = (0.5 * u * (1.0 + gelu_tanh(u))).astype(BF16)
    stream = (middle + dot(hidden, w_down[...])).astype(BF16).astype(F32)
    for j in range(TOGETHER):
        length = counts[step * TOGETHER + j]
        live = lax.broadcasted_iota(jnp.int32, (slots, width), 0) < length
        kept = jnp.where(live, stream[j * slots : (j + 1) * slots], 0.0)
        pooled_o[0, j : j + 1, :] = jnp.sum(kept, axis=0, keepdims=True)


def backward_kernel(
    counts, x_ref, bins_ref, proj_ref, att_ref, ctx_ref, mid_ref, back_ref, tail_ref,
    g1, w_qkv, w_out, g2, w_up, w_down,
    flat_o, table_acc,
):
    step = pl.program_id(0)
    slots = bins_ref.shape[1]
    width = x_ref.shape[1]
    ffn = w_up.shape[1]
    heads = att_ref.shape[2] // slots
    levels_n = table_acc.shape[0] // (8 * heads)
    scale = 1.0 / math.sqrt(width // heads)
    lanes = head_lanes(slots, width, heads)
    base_out = 3 * width
    base_up = base_out + width
    base_down = base_up + ffn
    base_phi = base_down + ffn
    base_tail = base_phi + width

    @pl.when(step == 0)
    def _():
        flat_o[...] = jnp.zeros(flat_o.shape, F32)
        table_acc[...] = jnp.zeros(table_acc.shape, F32)

    parts = []
    for j in range(TOGETHER):
        length = counts[step * TOGETHER + j]
        live = lax.broadcasted_iota(jnp.int32, (slots, width), 0) < length
        parts.append(jnp.where(live, back_ref[0, j : j + 1, :], 0.0))
    d_stream = jnp.concatenate(parts, axis=0)
    d_stream_b = d_stream.astype(BF16)
    middle = mid_ref[...]
    hat2, inverse2 = center(middle)
    normed2 = (hat2 * g2[...]).astype(BF16)
    d_normed = jnp.zeros(middle.shape, F32)
    for c in range(0, ffn, width):
        cols = slice(c, c + width)
        u = dot(normed2, w_up[:, cols])
        t = gelu_tanh(u)
        hidden = (0.5 * u * (1.0 + t)).astype(BF16)
        d_hidden = dot(d_stream_b, w_down[cols, :], 1, 1).astype(BF16).astype(F32)
        slope = 0.5 * (1.0 + t) + 0.5 * u * (1.0 - t * t) * (
            GELU_A * (1.0 + 3.0 * GELU_B * (u * u))
        )
        d_u = (d_hidden * slope).astype(BF16)
        flat_o[base_down + c : base_down + c + width, :] += dot(hidden, d_stream_b, 0, 0)
        flat_o[base_up + c : base_up + c + width, :] += dot(normed2, d_u, 0, 0)
        d_normed = d_normed + dot(d_u, w_up[:, cols], 1, 1)
    d_normed = d_normed.astype(BF16).astype(F32)
    flat_o[base_tail + 1 : base_tail + 2, :] += jnp.sum(d_normed * hat2, axis=0, keepdims=True)
    d_middle = d_stream_b.astype(F32) + center_back(d_normed * g2[...], hat2, inverse2)
    d_middle_b = d_middle.astype(BF16)
    d_context = dot(d_middle_b, w_out[...], 1, 1).astype(BF16)
    flat_o[base_out : base_out + width, :] += dot(ctx_ref[...], d_middle_b, 0, 0)

    d_rows = []
    for j in range(TOGETHER):
        rows = slice(j * slots, (j + 1) * slots)
        queries = spread(proj_ref[rows, 0:width], lanes)
        keys = proj_ref[rows, width : 2 * width]
        values = proj_ref[rows, 2 * width : 3 * width]
        d_ctx = spread(d_context[rows], lanes)
        attend = att_ref[j]
        d_att = dot(values, d_ctx, 1, 1)
        d_values = dot(attend, d_ctx)
        levels = bins_ref[j].T
        pieces = []
        for h in range(heads):
            cols = slice(h * slots, (h + 1) * slots)
            a = attend[:, cols].astype(F32)
            d_a = d_att[:, cols]
            inner = jnp.sum(a * d_a, axis=0, keepdims=True)
            d_s = a * (d_a - inner)
            for b in range(levels_n):
                held = jnp.where(levels == b, d_s, 0.0)
                at = (b * heads + h) * 8
                table_acc[at : at + 8, :] += jnp.sum(held.reshape(slots // 8, 8, slots), axis=0)
            pieces.append((d_s * scale).astype(BF16))
        d_score = jnp.concatenate(pieces, axis=1)
        d_keys = dot(d_score, queries)
        d_queries = collect(dot(d_score, keys, 0, 0), lanes, slots)
        d_rows.append(
            jnp.concatenate(
                [d_queries.astype(BF16), d_keys.astype(BF16), d_values.astype(BF16)], axis=1
            )
        )
    d_proj = jnp.concatenate(d_rows, axis=0)
    hat1, _ = center(x_ref[...].astype(F32))
    normed1 = (hat1 * g1[...]).astype(BF16)
    for c in range(3):
        cols = slice(c * width, (c + 1) * width)
        flat_o[c * width : (c + 1) * width, :] += dot(normed1, d_proj[:, cols], 0, 0)
    d_first = dot(d_proj, w_qkv[...], 1, 1).astype(BF16).astype(F32)
    flat_o[base_tail : base_tail + 1, :] += jnp.sum(d_first * hat1, axis=0, keepdims=True)

    @pl.when(step == pl.num_programs(0) - 1)
    def _():
        flat_o[0:base_phi, :] = flat_o[0:base_phi, :].astype(BF16).astype(F32)
        flat_o[base_phi:base_tail, :] = tail_ref[0:width, :]
        flat_o[base_tail + 2 : base_tail + 4, :] = tail_ref[width : width + 2, :]
        count = levels_n * heads
        flat_o[base_tail + 8 : base_tail + 8 + count, 0:slots] = jnp.sum(
            table_acc[...].reshape(count, 8, slots), axis=1
        )


def whole_block(shape):
    return pl.BlockSpec(shape, lambda i: (0,) * len(shape))


def row_block(shape):
    return pl.BlockSpec(shape, lambda i: (i,) + (0,) * (len(shape) - 1))


def flow_head(head_weights, summed, number, masses):
    w_mean, w_scale = head_weights
    average = summed / number[..., None]
    centre = jnp.sum(average * w_mean, axis=-1)
    log_width = jnp.sum(average * w_scale, axis=-1)
    return 0.5 * jnp.square((masses - centre) * jnp.exp(-log_width)) + log_width


def total_over_all(flat):
    return lax.psum(flat, ("dp", "ens"))


def shards(
    embed, counts, member, bins, masses,
    gain_attn, w_qkv, w_out, pair_table, gain_ffn, w_up, w_down, w_phi, w_mean, w_scale,
):
    jets_n, slots, width = embed.shape[1:]
    heads = pair_table.shape[2]
    levels_n = pair_table.shape[1]
    ffn = w_up.shape[2]
    lengths = counts[0]
    pair_bins = bins[0]
    group_masses = masses[0]
    groups_total = group_masses.shape[0]
    steps = jets_n // TOGETHER
    block = TOGETHER * slots
    x = embed[0].reshape(jets_n * slots, width)
    weights = (gain_attn, w_qkv[0], w_out[0], gain_ffn, w_up[0], w_down[0])
    weight_specs = [whole_block(w.shape) for w in weights]
    smem = pl.BlockSpec(memory_space=pltpu.SMEM)
    params = pltpu.CompilerParams(
        dimension_semantics=("arbitrary",), vmem_limit_bytes=50 * 1024 * 1024
    )
    bins_spec = row_block((TOGETHER, slots, slots))
    kept_specs = [
        row_block((block, 3 * width)),
        row_block((TOGETHER, slots, heads * slots)),
        row_block((block, width)),
        row_block((block, width)),
    ]
    proj, att, ctx, mid, pooled_sum = pl.pallas_call(
        forward_kernel,
        grid=(steps,),
        in_specs=[smem, smem, row_block((block, width)), bins_spec] + weight_specs,
        out_specs=kept_specs + [row_block((1, TOGETHER, width))],
        out_shape=[
            jax.ShapeDtypeStruct((jets_n * slots, 3 * width), BF16),
            jax.ShapeDtypeStruct((jets_n, slots, heads * slots), BF16),
            jax.ShapeDtypeStruct((jets_n * slots, width), BF16),
            jax.ShapeDtypeStruct((jets_n * slots, width), F32),
            jax.ShapeDtypeStruct((steps, TOGETHER, width), F32),
        ],
        compiler_params=params,
        name="forward",
    )(lengths, pair_table[0], x, pair_bins, *weights)

    inverse_length = lengths[:, None].astype(F32)
    pooled = (pooled_sum.reshape(jets_n, width) / inverse_length).astype(BF16)

    def phi_part(pooled_in, w_in):
        return jax.nn.gelu(jnp.dot(pooled_in, w_in, preferred_element_type=F32))

    phi, back_phi = jax.vjp(phi_part, pooled, w_phi)
    group_onehot = (member[0][:, None] == jnp.arange(groups_total, dtype=jnp.int32)).astype(F32)
    partial_sum = jnp.dot(group_onehot.T, phi, precision=lax.Precision.HIGHEST)
    tally = jnp.sum(group_onehot, axis=0)
    joined = jnp.concatenate(
        [partial_sum, jnp.broadcast_to(tally[:, None], (groups_total, 128))], axis=1
    )
    joined = lax.psum(joined, "ens")
    summed, number = joined[:, :width], joined[:, width]

    def head_part(head_weights, summed_in):
        return flow_head(head_weights, summed_in, number, group_masses)

    neg_loglik, back_head = jax.vjp(head_part, (w_mean, w_scale), summed)
    scale_total = 1.0 / (lax.axis_size("dp") * groups_total)
    head_grads, summed_grad = back_head(jnp.full(neg_loglik.shape, scale_total, F32))
    phi_grad = jnp.dot(group_onehot, summed_grad, precision=lax.Precision.HIGHEST)
    d_pooled, d_phi = back_phi(phi_grad)
    d_pooled = (d_pooled.astype(F32) / inverse_length).reshape(steps, TOGETHER, width)
    share = 1.0 / lax.axis_size("ens")
    tail = jnp.concatenate(
        [
            d_phi.astype(F32),
            head_grads[0][None] * share,
            head_grads[1][None] * share,
            jnp.zeros((6, width), F32),
        ],
        axis=0,
    )

    base_tail = 3 * width + width + 2 * ffn + width
    unit = 8 * lax.axis_size("dp") * lax.axis_size("ens")
    used = base_tail + 8 + levels_n * heads
    flat_rows = (used + unit - 1) // unit * unit
    flat = pl.pallas_call(
        backward_kernel,
        grid=(steps,),
        in_specs=[smem, row_block((block, width)), bins_spec]
        + kept_specs
        + [row_block((1, TOGETHER, width)), whole_block(tail.shape)]
        + weight_specs,
        out_specs=whole_block((flat_rows, width)),
        out_shape=jax.ShapeDtypeStruct((flat_rows, width), F32),
        scratch_shapes=[pltpu.VMEM((levels_n * heads * 8, slots), F32)],
        compiler_params=params,
        name="backward",
    )(lengths, x, pair_bins, proj, att, ctx, mid, d_pooled, tail, *weights)

    total = total_over_all(flat)
    g_qkv = jnp.concatenate([total[i * width : (i + 1) * width] for i in range(3)], axis=1)
    at = 3 * width
    g_out = total[at : at + width]
    at += width
    g_up = jnp.concatenate(
        [total[at + i : at + i + width] for i in range(0, ffn, width)], axis=1
    )
    at += ffn
    g_down = total[at : at + ffn]
    at += ffn
    g_phi = total[at : at + width]
    small = total[base_tail : base_tail + 8 + levels_n * heads]
    g_table = jnp.sum(small[8:, :slots], axis=1).reshape(1, levels_n, heads)
    return (
        neg_loglik[None, :],
        small[0:1],
        g_qkv[None],
        g_out[None],
        g_table,
        small[1:2],
        g_up[None],
        g_down[None],
        g_phi,
        small[2],
        small[3],
    )


def solution(mesh):
    in_specs = (
        P("dp", "ens", None, None),
        P("dp", "ens"),
        P("dp", "ens"),
        P("dp", "ens", None, None),
        P("dp", None),
    ) + (P(),) * 10
    out_specs = (P("dp", None),) + (P(),) * 10
    return jax.shard_map(shards, mesh=mesh, in_specs=in_specs, out_specs=out_specs, check_vma=False)
```

profile of v0, /device:TPU:0, one launch (start us, length us, event | category | flops | bytes accessed | tf_op | source)
XLA Modules:
  0.0 262.5 jit_solution(12662194551866377550)
XLA Ops:
  7.2 0.0 copy-start
  7.2 0.0 copy-start.19
  7.2 0.0 copy-start.23
  7.2 0.0 copy-start.17
  7.2 0.0 copy-start.15
  7.3 0.0 all-reduce.2.cloned.1.call-start
  7.3 0.7 bitcast_convert_fusion
  8.0 0.8 convert_reduce_fusion
  8.8 1.2 copy-done.1
  10.0 1.0 copy-done.4
  11.1 1.0 copy-done.6
  12.1 1.0 copy-done.8
  13.1 0.9 copy-done.11
  14.0 0.7 copy-done.13
  14.7 0.7 copy-done.14
  15.4 0.7 copy-done.16
  16.0 0.7 copy-done.18
  16.7 23.1 %forward.1 = (bf16[2048,768]{1,0:T(8,128)(2,1)}, bf16[16,128,1024]{2,1,0:T(8,128)(2,1)}, bf16[2048,256]{1,0:T(8,128)(2,1)S(1)}, f32[2048,256]{1,0:T(8,128)}, f32[8,2,256]{2,1,0:T(2,128)S(1)}) custom-call(s32[16]{0:T(128)S(1)} %bitcast.62, f32[8,8]{1,0:T(8,128)S(1)} %bitcast.61, bf16[2048,256]{1,0:T(8,128)(2,1)S(1)} %bitcast.49, s32[16,128,128]{2,1,0:T(8,128)} %bitcast.51, ...), custom_call_target="tpu_custom_call" | custom-call | tf_op jit(solution)/shard_map/forward/pallas_call | solution.py:267
  39.8 1.0 copy-done.10
  40.8 0.2 fusion.36
  41.0 0.1 fusion.9
  41.2 0.1 broadcast_in_dim.16
  41.2 23.4 %psum.14 = f32[4,384]{1,0:T(4,128)S(1)} all-reduce(f32[4,384]{1,0:T(4,128)S(1)} %pad_maximum_fusion), channel_id=1, replica_groups=mesh['dp'=4,'ens'=8] {'ens'}, use_global_device_ids=true, to_apply=%region_1.0 | all-reduce | flops 1536 | bytes 12288 | tf_op jit(solution)/shard_map/psum | solution.py:296
  64.6 0.1 slice_reduce_fusion.1
  64.7 0.2 multiply_reduce_fusion.3
  65.0 0.2 fusion.8
  65.2 0.2 fusion.2
  65.3 1.0 fusion
  66.4 0.1 multiply_reduce_fusion.1
  66.5 0.1 pad.10.clone
  66.6 1.0 maximum_maximum_fusion.tail_ref
  67.6 0.0 copy-done.19
  67.6 0.0 copy-done.17
  67.6 0.0 copy-done.15
  67.7 0.0 copy-done.2
  67.7 0.0 copy-start.9
  67.7 1.0 copy-done.9
  68.7 40.4 %backward.1 = f32[3584,256]{1,0:T(8,128)} custom-call(s32[16]{0:T(128)S(1)} %bitcast.63, bf16[2048,256]{1,0:T(8,128)(2,1)S(1)} %bitcast.50, s32[16,128,128]{2,1,0:T(8,128)S(1)} %bitcast.52, bf16[2048,768]{1,0:T(8,128)(2,1)} %get-tuple-element.17.proj_ref, bf16[16,128,1024]{2,1,0:T(8,128)(2,1)} %get-tuple-element.18.att_ref, bf16[2048,256]{1,0:T(8,128)(2,1)} %copy-done.10, ...), custom_call_target="tpu_custom_call" | custom-call | tf_op jit(solution)/shard_map/backward/pallas_call | solution.py:323
  109.1 0.0 all-reduce.2.cloned.1.call-update
  109.1 0.5 bitcast_add_fusion
  109.6 136.3 %all-reduce.2.cloned.1.call-done = f32[3584,256]{1,0:T(8,128)} async-done(((f32[3584,256]{1,0:T(8,128)}), f32[3584,256]{1,0:T(8,128)}) %all-reduce.2.cloned.1.call-update) | async-done | bytes 3670032 | tf_op jit(solution)/shard_map/psum | solution.py:236
  245.9 0.9 slice_reduce_fusion
  246.8 0.7 reshape.81
  247.5 2.5 fusion.38
  250.0 0.9 maximum_bitcast_fusion.1
  250.9 1.1 maximum_bitcast_fusion
  252.0 1.4 fusion.37
  253.4 2.3 slice_bitcast_fusion
  (33 shorter events, 0.1 us)
Async XLA Ops:
  7.2 33.6 %copy-start = (bf16[256,256]{1,0:T(8,128)(2,1)S(1)}, bf16[256,256]{1,0:T(8,128)(2,1)}, u32[]{:S(2)}) copy-start(bf16[256,256]{1,0:T(8,128)(2,1)} %param.27) | copy-start | bytes 393220
  7.2 60.4 %copy-start.19 = (s32[1,16]{1,0:T(1,128)S(1)}, s32[1,16]{1,0:T(1,128)}, u32[]{:S(2)}) copy-start(s32[1,16]{1,0:T(1,128)} %param.16) | copy-start | bytes 196
  7.2 33.8 %copy-start.23 = (s32[1,16]{1,0:T(1,128)S(1)}, s32[1,16]{1,0:T(1,128)}, u32[]{:S(2)}) copy-start(s32[1,16]{1,0:T(1,128)} %param.17) | copy-start | bytes 196
  7.2 60.4 %copy-start.17 = (f32[1,256]{1,0:T(1,128)S(1)}, f32[1,256]{1,0:T(1,128)}, u32[]{:S(2)}) copy-start(f32[1,256]{1,0:T(1,128)} %g2.3) | copy-start | bytes 3076
  7.2 60.4 %copy-start.15 = (f32[1,256]{1,0:T(1,128)S(1)}, f32[1,256]{1,0:T(1,128)}, u32[]{:S(2)}) copy-start(f32[1,256]{1,0:T(1,128)} %g1.3) | copy-start | bytes 3076
  7.2 57.5 %copy-start.22 = (f32[256]{0:T(256)S(1)}, f32[256]{0:T(256)}, u32[]{:S(2)}) copy-start(f32[256]{0:T(256)} %param.29) | copy-start | bytes 3076
  7.3 57.5 %copy-start.21 = (f32[256]{0:T(256)S(1)}, f32[256]{0:T(256)}, u32[]{:S(2)}) copy-start(f32[256]{0:T(256)} %param.28) | copy-start | bytes 3076
  7.3 57.7 %copy-start.20 = (f32[1,4]{1,0:T(1,128)S(1)}, f32[1,4]{1,0:T(1,128)}, u32[]{:S(2)}) copy-start(f32[1,4]{1,0:T(1,128)} %param.19) | copy-start | bytes 52
  7.3 238.7 %all-reduce.2.cloned.1.call-start = ((), (), s32[]{:S(2)}) async-start(), calls=%async_computation | async-start | bytes 7340032 | tf_op jit(solution)/shard_map/psum | solution.py:236
  8.8 1.2 copy-start.1
  10.0 1.0 copy-start.4
  11.1 1.0 copy-start.6
  12.1 1.0 copy-start.8
  13.1 0.9 copy-start.11
  14.0 0.7 copy-start.13
  14.7 0.7 copy-start.14
  15.4 0.7 copy-start.16
  16.0 0.7 copy-start.18
  16.7 51.0 %copy-start.2 = (bf16[1,16,128,256]{3,2,1,0:T(8,128)(2,1)S(1)}, bf16[1,16,128,256]{3,2,1,0:T(8,128)(2,1)}, u32[]{:S(2)}) copy-start(bf16[1,16,128,256]{3,2,1,0:T(8,128)(2,1)} %param.15) | copy-start | bytes 3145732
  16.7 51.0 %copy-start.3 = (s32[1,16,128,128]{3,2,1,0:T(8,128)S(1)}, s32[1,16,128,128]{3,2,1,0:T(8,128)}, u32[]{:S(2)}) copy-start(s32[1,16,128,128]{3,2,1,0:T(8,128)} %param.18) | copy-start | bytes 3145732
  16.7 51.0 %copy-start.5 = (bf16[1,256,1024]{2,1,0:T(8,128)(2,1)S(1)}, bf16[1,256,1024]{2,1,0:T(8,128)(2,1)}, u32[]{:S(2)}) copy-start(bf16[1,256,1024]{2,1,0:T(8,128)(2,1)} %param.25) | copy-start | bytes 1572868
  16.7 51.0 %copy-start.7 = (bf16[1,1024,256]{2,1,0:T(8,128)(2,1)S(1)}, bf16[1,1024,256]{2,1,0:T(8,128)(2,1)}, u32[]{:S(2)}) copy-start(bf16[1,1024,256]{2,1,0:T(8,128)(2,1)} %param.26) | copy-start | bytes 1572868
  16.7 51.0 %copy-start.12 = (bf16[1,256,256]{2,1,0:T(8,128)(2,1)S(1)}, bf16[1,256,256]{2,1,0:T(8,128)(2,1)}, u32[]{:S(2)}) copy-start(bf16[1,256,256]{2,1,0:T(8,128)(2,1)} %param.22) | copy-start | bytes 393220
  39.8 1.0 copy-start.10
  67.7 1.0 copy-start.9
Sparse Core Ops, SparseCore 0:
  109.2 136.6 all-reduce.1
where the time goes:
time: 263 us
  waiting for transfers between devices  136 us (52%)
  Pallas kernels  63.5 us (24%)
  blocking collectives  23.4 us (9%)
  local copies, waits for them, and re-layouts  17.1 us (7%)
  between operations  14.3 us (5%)
  other arithmetic  6.22 us (2%)
    psum x1, waiting for transfers between devices, total_over_all(): return lax.psum(flat, ('dp', 'ens'))  136 us
    pallas_call x1, Pallas kernels, shards(): pl.pallas_call(backward_kernel, grid=(steps,), in_specs=[smem, row_block(...  40.4 us
    psum x1, blocking collectives, shards(): joined = lax.psum(joined, 'ens')  23.4 us
    pallas_call x1, Pallas kernels, shards(): pl.pallas_call(forward_kernel, grid=(steps,), in_specs=[smem, smem, row_b...  23.1 us
    unnamed x48, local copies, waits for them, and re-layouts  9.93 us
  transfers between devices with their start and end apart: 1, of which 1 were waited for; matrix products, arithmetic and copies ran while one was open for 0% of the time, Pallas kernels for 0%

commit v1 on v0

--- a/solution.py
+++ b/solution.py
@@ -232,8 +232,170 @@
     return 0.5 * jnp.square((masses - centre) * jnp.exp(-log_width)) + log_width
 
 
+MESH = pl.DeviceIdType.MESH
+
+
+def greet(partners):
+    barrier = pltpu.get_barrier_semaphore()
+    for partner in partners:
+        pl.semaphore_signal(barrier, inc=1, device_id=partner, device_id_type=MESH)
+    pl.semaphore_wait(barrier, len(partners))
+
+
+def reduce_kernel(ens, x_ref, out_ref, work, full, in_a, in_b, in_c, in_d, send, recv, own):
+    d, e = lax.axis_index("dp"), lax.axis_index("ens")
+    core, xb = d % 2, d // 2
+    yb, z = e % 2, e // 2
+    line = ens // 2
+    rows = x_ref.shape[0]
+    size_a, size_b, size_c = rows // 2, rows // 4, rows // 8
+    size_d = size_c // line
+
+    def span(start, size):
+        return pl.ds(pl.multiple_of(start, 8), size)
+
+    bit_b = (1 - core) * xb + core * yb
+    bit_c = (1 - core) * yb + core * xb
+    step_x = 2 * (1 - 2 * xb)
+    step_y = 1 - 2 * yb
+    mate_a = (d + 1 - 2 * core, e)
+    mate_b = (d + (1 - core) * step_x, e + core * step_y)
+    mate_c = (d + core * step_x, e + (1 - core) * step_y)
+    mates_d = [(d, (z + k) % line * 2 + yb) for k in range(1, line)]
+    greet([mate_a, mate_b, mate_c] + mates_d)
+
+    def copy(source, target, number, mate):
+        return pltpu.make_async_remote_copy(
+            src_ref=source, dst_ref=target, send_sem=send.at[number], recv_sem=recv.at[number],
+            device_id=mate, device_id_type=MESH,
+        )
+
+    start_a = core * size_a
+    start_b = start_a + bit_b * size_b
+    start_c = start_b + bit_c * size_c
+    start_d = start_c + z * size_d
+
+    there = copy(x_ref.at[span((1 - core) * size_a, size_a)], in_a, 0, mate_a)
+    there.start()
+    there.wait()
+    part = span(start_a, size_a)
+    work[part, :] = x_ref[part, :] + in_a[...]
+
+    there = copy(work.at[span(start_a + (1 - bit_b) * size_b, size_b)], in_b, 1, mate_b)
+    there.start()
+    there.wait()
+    part = span(start_b, size_b)
+    work[part, :] = work[part, :] + in_b[...]
+
+    there = copy(work.at[span(start_b + (1 - bit_c) * size_c, size_c)], in_c, 2, mate_c)
+    there.start()
+    there.wait()
+    part = span(start_c, size_c)
+    work[part, :] = work[part, :] + in_c[...]
+
+    group = []
+    for k in range(1, line):
+        piece = span(start_c + (z + k) % line * size_d, size_d)
+        group.append(copy(work.at[piece], in_d.at[k - 1], 2 + k, mates_d[k - 1]))
+    for there in group:
+        there.start()
+    for there in group:
+        there.wait()
+    part = span(start_d, size_d)
+    total = work[part, :]
+    for k in range(1, line):
+        total = total + in_d[k - 1]
+    full[part, :] = total
+
+    group = [
+        copy(full.at[part], full.at[part], 1 + line + k, mates_d[k - 1]) for k in range(1, line)
+    ]
+    for there in group:
+        there.start()
+    for there in group:
+        there.wait()
+    last = 2 * line + 1
+    for number, start, size, mate in (
+        (last, start_c, size_c, mate_c),
+        (last + 1, start_b, size_b, mate_b),
+        (last + 2, start_a, size_a, mate_a),
+    ):
+        part = span(start, size)
+        there = copy(full.at[part], full.at[part], number, mate)
+        there.start()
+        there.wait()
+    back = pltpu.make_async_copy(full, out_ref, own)
+    back.start()
+    back.wait()
+
+
 def total_over_all(flat):
-    return lax.psum(flat, ("dp", "ens"))
+    ens = lax.axis_size("ens")
+    rows, width = flat.shape
+    line = ens // 2
+    count = 2 * line + 4
+    return pl.pallas_call(
+        functools.partial(reduce_kernel, ens),
+        out_shape=jax.ShapeDtypeStruct(flat.shape, F32),
+        in_specs=[pl.BlockSpec(memory_space=pltpu.VMEM)],
+        out_specs=pl.BlockSpec(memory_space=pl.ANY),
+        scratch_shapes=[
+            pltpu.VMEM((rows, width), F32),
+            pltpu.VMEM((rows, width), F32),
+            pltpu.VMEM((rows // 2, width), F32),
+            pltpu.VMEM((rows // 4, width), F32),
+            pltpu.VMEM((rows // 8, width), F32),
+            pltpu.VMEM((line - 1, rows // 8 // line, width), F32),
+            pltpu.SemaphoreType.DMA((count,)),
+            pltpu.SemaphoreType.DMA((count,)),
+            pltpu.SemaphoreType.DMA,
+        ],
+        compiler_params=pltpu.CompilerParams(
+            collective_id=0, has_side_effects=True, vmem_limit_bytes=40 * 1024 * 1024
+        ),
+        name="reduce",
+    )(flat)
+
+
+def small_kernel(ens, x_ref, out_ref, slots, send, recv):
+    d, e = lax.axis_index("dp"), lax.axis_index("ens")
+    mates = [(d, (e + k) % ens) for k in range(1, ens)]
+    greet(mates)
+    copies = []
+    for k in range(1, ens):
+        copies.append(
+            pltpu.make_async_remote_copy(
+                src_ref=x_ref, dst_ref=slots.at[e], send_sem=send.at[k], recv_sem=recv.at[k],
+                device_id=mates[k - 1], device_id_type=MESH,
+            )
+        )
+    for there in copies:
+        there.start()
+    slots[e] = x_ref[...]
+    for there in copies:
+        there.wait()
+    total = slots[0]
+    for i in range(1, ens):
+        total = total + slots[i]
+    out_ref[...] = total
+
+
+def total_over_ens(rows):
+    ens = lax.axis_size("ens")
+    vmem = pl.BlockSpec(memory_space=pltpu.VMEM)
+    return pl.pallas_call(
+        functools.partial(small_kernel, ens),
+        out_shape=jax.ShapeDtypeStruct(rows.shape, F32),
+        in_specs=[vmem],
+        out_specs=vmem,
+        scratch_shapes=[
+            pltpu.VMEM((ens,) + rows.shape, F32),
+            pltpu.SemaphoreType.DMA((ens,)),
+            pltpu.SemaphoreType.DMA((ens,)),
+        ],
+        compiler_params=pltpu.CompilerParams(collective_id=1, has_side_effects=True),
+        name="small",
+    )(rows)
 
 
 def shards(
@@ -293,7 +455,8 @@
     joined = jnp.concatenate(
         [partial_sum, jnp.broadcast_to(tally[:, None], (groups_total, 128))], axis=1
     )
-    joined = lax.psum(joined, "ens")
+    joined = jnp.concatenate([joined, jnp.zeros((-groups_total % 8, joined.shape[1]), F32)], axis=0)
+    joined = total_over_ens(joined)[:groups_total]
     summed, number = joined[:, :width], joined[:, width]
 
     def head_part(head_weights, summed_in):

time: 263 us -> 177 us (0.67)
  waiting for transfers between devices: 136 us -> 0 us
  Pallas kernels: 63.5 us -> 147 us
  blocking collectives: 23.4 us -> 0 us
  between operations: 14.3 us -> 0.9 us
  local copies, waits for them, and re-layouts: 17.1 us -> 21.6 us
    psum x1 -> x0, waiting for transfers between devices: 136 us -> none  [total_over_all(): return lax.psum(flat, ('dp', 'ens'))]
    pallas_call x0 -> x2, Pallas kernels: none -> 83.2 us  [the longest x1 73 us: total_over_all(): pl.pallas_call(functools.partial(reduce_kernel, ens), out_shape=jax.Shape...]
    psum x1 -> x0, blocking collectives: 23.4 us -> none  [shards(): joined = lax.psum(joined, 'ens')]
    unnamed x48 -> x52, local copies, waits for them, and re-layouts: 9.93 us -> 13.8 us
  transfers between devices with their start and end apart: 1 -> 0, of which waited for: 1 -> 0; matrix products, arithmetic and copies ran while one was open for 0% -> 0% of each run, Pallas kernels for 0% -> 0%
where the time goes in v1:
time: 177 us; the launch traced here: 176 us
  Pallas kernels  147 us (83%)
  local copies, waits for them, and re-layouts  21.6 us (12%)
  other arithmetic  5.89 us (3%)
    pallas_call x1, Pallas kernels, total_over_all(): pl.pallas_call(functools.partial(reduce_kernel, ens), out_shape=jax.Shape...  73 us
    pallas_call x1, Pallas kernels, shards(): pl.pallas_call(backward_kernel, grid=(steps,), in_specs=[smem, row_block(...  40.4 us
    pallas_call x1, Pallas kernels, shards(): pl.pallas_call(forward_kernel, grid=(steps,), in_specs=[smem, smem, row_b...  23.1 us
    unnamed x52, local copies, waits for them, and re-layouts  13.8 us
    pallas_call x1, Pallas kernels, total_over_ens(): pl.pallas_call(functools.partial(small_kernel, ens), out_shape=jax.ShapeD...  10.2 us

profile of v1, /device:TPU:0, one launch (start us, length us, event | category | flops | bytes accessed | tf_op | source)
XLA Modules:
  0.0 176.1 jit_solution(14986013737363239780)
XLA Ops:
  0.6 0.0 copy-start
  0.7 0.0 copy-start.19
  0.7 0.0 copy-start.17
  0.7 0.0 copy-start.21
  0.7 0.0 copy-start.25
  0.7 0.7 bitcast_convert_fusion
  1.5 0.8 convert_reduce_fusion
  2.2 0.1 pad.11.clone
  2.3 0.1 broadcast_in_dim.16
  2.4 1.2 copy-done.3
  3.6 1.0 copy-done.6
  4.7 1.0 copy-done.8
  5.7 1.0 copy-done.10
  6.7 0.9 copy-done.13
  7.6 0.7 copy-done.15
  8.3 0.7 copy-done.16
  9.0 0.7 copy-done.18
  9.6 0.7 copy-done.20
  10.3 23.1 %forward.1 = (bf16[2048,768]{1,0:T(8,128)(2,1)}, bf16[16,128,1024]{2,1,0:T(8,128)(2,1)}, bf16[2048,256]{1,0:T(8,128)(2,1)S(1)}, f32[2048,256]{1,0:T(8,128)}, f32[8,2,256]{2,1,0:T(2,128)S(1)}) custom-call(s32[16]{0:T(128)S(1)} %bitcast.62, f32[8,8]{1,0:T(8,128)S(1)} %bitcast.61, bf16[2048,256]{1,0:T(8,128)(2,1)S(1)} %bitcast.49, s32[16,128,128]{2,1,0:T(8,128)} %bitcast.51, ...), custom_call_target="tpu_custom_call" | custom-call | tf_op jit(solution)/shard_map/forward/pallas_call | solution.py:429
  33.4 1.0 copy-done.12
  34.4 0.0 copy-done
  34.4 0.2 fusion.36
  34.6 0.1 fusion.9
  34.7 0.6 select_maximum_fusion.x_ref
  35.3 10.2 %small.1 = f32[8,384]{1,0:T(8,128)} custom-call(f32[8,384]{1,0:T(8,128)} %select_maximum_fusion.x_ref), custom_call_target="tpu_custom_call" | custom-call | tf_op jit(solution)/shard_map/small/pallas_call | solution.py:386
  45.6 0.8 slice_reduce_fusion.1
  46.4 0.0 copy-done.23
  46.4 0.9 multiply_reduce_fusion.3
  47.3 0.5 bitcast_add_fusion
  47.8 0.2 fusion.8
  48.1 0.1 multiply_reduce_fusion.1
  48.2 0.2 fusion.2
  48.4 0.3 fusion
  48.7 0.1 maximum_maximum_fusion.tail_ref
  48.8 0.0 copy-done.19
  48.9 0.0 copy-start.11
  48.9 1.0 copy-done.11
  49.9 40.4 %backward.1.x_ref = f32[3584,256]{1,0:T(8,128)} custom-call(s32[16]{0:T(128)S(1)} %bitcast.63, bf16[2048,256]{1,0:T(8,128)(2,1)S(1)} %bitcast.50, s32[16,128,128]{2,1,0:T(8,128)S(1)} %bitcast.52, bf16[2048,768]{1,0:T(8,128)(2,1)} %get-tuple-element.17.proj_ref, bf16[16,128,1024]{2,1,0:T(8,128)(2,1)} %get-tuple-element.18.att_ref, ...), custom_call_target="tpu_custom_call" | custom-call | tf_op jit(solution)/shard_map/backward/pallas_call | solution.py:486
  90.2 2.0 %copy-done.1 = f32[3584,256]{1,0:T(8,128)S(1)} copy-done((f32[3584,256]{1,0:T(8,128)S(1)}, f32[3584,256]{1,0:T(8,128)}, u32[]{:S(2)}) %copy-start.1) | copy-done | bytes 3670040
  92.3 73.0 %reduce.3 = f32[3584,256]{1,0:T(8,128)S(1)} custom-call(f32[3584,256]{1,0:T(8,128)S(1)} %copy-done.1), custom_call_target="tpu_custom_call" | custom-call | tf_op jit(solution)/shard_map/reduce/pallas_call | solution.py:337
  165.3 1.8 %copy-done.2 = f32[3584,256]{1,0:T(8,128)} copy-done((f32[3584,256]{1,0:T(8,128)}, f32[3584,256]{1,0:T(8,128)S(1)}, u32[]{:S(2)}) %copy-start.2) | copy-done | bytes 3670040
  167.1 0.1 slice_reduce_fusion
  167.2 0.7 reshape.81
  167.8 1.4 fusion.37
  169.3 2.3 %slice_bitcast_fusion = f32[1,1024,256]{2,1,0:T(8,128)} fusion(f32[3584,256]{1,0:T(8,128)} %copy-done.2), kind=kLoop, calls=%fused_computation.6 | loop fusion | bytes 2097152 | tf_op jit(solution)/shard_map/broadcast_in_dim | solution.py:522
  171.5 2.5 %fusion.38 = (f32[256,256]{1,0:T(8,128)}, f32[256,256]{1,0:T(8,128)S(1)}, f32[256,256]{1,0:T(8,128)S(1)}, f32[256,256]{1,0:T(8,128)S(1)}, f32[256,256]{1,0:T(8,1...) fusion(f32[3584,256]{1,0:T(8,128)} %copy-done.2), kind=kLoop, calls=%fused_computation.69 | loop fusion | bytes 4718592 | tf_op jit(solution)/shard_map/slice | solution.py:511
  174.1 0.9 maximum_bitcast_fusion.1
  175.0 1.1 maximum_bitcast_fusion
  (35 shorter events, 0.1 us)
Async XLA Ops:
  0.6 33.7 %copy-start = (bf16[256,256]{1,0:T(8,128)(2,1)S(1)}, bf16[256,256]{1,0:T(8,128)(2,1)}, u32[]{:S(2)}) copy-start(bf16[256,256]{1,0:T(8,128)(2,1)} %param.27) | copy-start | bytes 393220
  0.7 45.7 %copy-start.24 = (f32[256]{0:T(256)S(1)}, f32[256]{0:T(256)}, u32[]{:S(2)}) copy-start(f32[256]{0:T(256)} %param.29) | copy-start | bytes 3076
  0.7 45.7 %copy-start.23 = (f32[256]{0:T(256)S(1)}, f32[256]{0:T(256)}, u32[]{:S(2)}) copy-start(f32[256]{0:T(256)} %param.28) | copy-start | bytes 3076
  0.7 48.1 %copy-start.19 = (f32[1,256]{1,0:T(1,128)S(1)}, f32[1,256]{1,0:T(1,128)}, u32[]{:S(2)}) copy-start(f32[1,256]{1,0:T(1,128)} %g2.3) | copy-start | bytes 3076
  0.7 48.1 %copy-start.17 = (f32[1,256]{1,0:T(1,128)S(1)}, f32[1,256]{1,0:T(1,128)}, u32[]{:S(2)}) copy-start(f32[1,256]{1,0:T(1,128)} %g1.3) | copy-start | bytes 3076
  0.7 46.6 %copy-start.22 = (f32[1,4]{1,0:T(1,128)S(1)}, f32[1,4]{1,0:T(1,128)}, u32[]{:S(2)}) copy-start(f32[1,4]{1,0:T(1,128)} %param.19) | copy-start | bytes 52
  0.7 48.1 %copy-start.21 = (s32[1,16]{1,0:T(1,128)S(1)}, s32[1,16]{1,0:T(1,128)}, u32[]{:S(2)}) copy-start(s32[1,16]{1,0:T(1,128)} %param.16) | copy-start | bytes 196
  0.7 33.8 %copy-start.25 = (s32[1,16]{1,0:T(1,128)S(1)}, s32[1,16]{1,0:T(1,128)}, u32[]{:S(2)}) copy-start(s32[1,16]{1,0:T(1,128)} %param.17) | copy-start | bytes 196
  2.4 1.2 copy-start.3
  3.6 1.0 copy-start.6
  4.6 1.0 copy-start.8
  5.7 1.0 copy-start.10
  6.7 0.9 copy-start.13
  7.6 0.7 copy-start.15
  8.3 0.7 copy-start.16
  9.0 0.7 copy-start.18
  9.6 0.7 copy-start.20
  10.3 38.5 %copy-start.4 = (bf16[1,16,128,256]{3,2,1,0:T(8,128)(2,1)S(1)}, bf16[1,16,128,256]{3,2,1,0:T(8,128)(2,1)}, u32[]{:S(2)}) copy-start(bf16[1,16,128,256]{3,2,1,0:T(8,128)(2,1)} %param.15) | copy-start | bytes 3145732
  10.3 38.5 %copy-start.5 = (s32[1,16,128,128]{3,2,1,0:T(8,128)S(1)}, s32[1,16,128,128]{3,2,1,0:T(8,128)}, u32[]{:S(2)}) copy-start(s32[1,16,128,128]{3,2,1,0:T(8,128)} %param.18) | copy-start | bytes 3145732
  10.3 38.5 %copy-start.7 = (bf16[1,256,1024]{2,1,0:T(8,128)(2,1)S(1)}, bf16[1,256,1024]{2,1,0:T(8,128)(2,1)}, u32[]{:S(2)}) copy-start(bf16[1,256,1024]{2,1,0:T(8,128)(2,1)} %param.25) | copy-start | bytes 1572868
  10.3 38.6 %copy-start.9 = (bf16[1,1024,256]{2,1,0:T(8,128)(2,1)S(1)}, bf16[1,1024,256]{2,1,0:T(8,128)(2,1)}, u32[]{:S(2)}) copy-start(bf16[1,1024,256]{2,1,0:T(8,128)(2,1)} %param.26) | copy-start | bytes 1572868
  10.3 38.6 %copy-start.14 = (bf16[1,256,256]{2,1,0:T(8,128)(2,1)S(1)}, bf16[1,256,256]{2,1,0:T(8,128)(2,1)}, u32[]{:S(2)}) copy-start(bf16[1,256,256]{2,1,0:T(8,128)(2,1)} %param.22) | copy-start | bytes 393220
  33.4 1.0 copy-start.12
  48.9 1.0 copy-start.11
  90.2 2.0 %copy-start.1 = (f32[3584,256]{1,0:T(8,128)S(1)}, f32[3584,256]{1,0:T(8,128)}, u32[]{:S(2)}) copy-start(f32[3584,256]{1,0:T(8,128)} %backward.1.x_ref) | copy-start | bytes 11010052
  165.3 1.8 %copy-start.2 = (f32[3584,256]{1,0:T(8,128)}, f32[3584,256]{1,0:T(8,128)S(1)}, u32[]{:S(2)}) copy-start(f32[3584,256]{1,0:T(8,128)S(1)} %reduce.3) | copy-start | bytes 11010052

commit v2 on v1

--- a/solution.py
+++ b/solution.py
@@ -247,9 +247,10 @@
     core, xb = d % 2, d // 2
     yb, z = e % 2, e // 2
     line = ens // 2
-    rows = x_ref.shape[0]
-    size_a, size_b, size_c = rows // 2, rows // 4, rows // 8
+    half = x_ref.shape[0] // 2
+    size_a, size_b, size_c = half // 2, half // 4, half // 8
     size_d = size_c // line
+    count = 2 * line + 4
 
     def span(start, size):
         return pl.ds(pl.multiple_of(start, 8), size)
@@ -270,60 +271,74 @@
             device_id=mate, device_id_type=MESH,
         )
 
-    start_a = core * size_a
-    start_b = start_a + bit_b * size_b
-    start_c = start_b + bit_c * size_c
-    start_d = start_c + z * size_d
-
-    there = copy(x_ref.at[span((1 - core) * size_a, size_a)], in_a, 0, mate_a)
-    there.start()
-    there.wait()
-    part = span(start_a, size_a)
-    work[part, :] = x_ref[part, :] + in_a[...]
-
-    there = copy(work.at[span(start_a + (1 - bit_b) * size_b, size_b)], in_b, 1, mate_b)
-    there.start()
-    there.wait()
-    part = span(start_b, size_b)
-    work[part, :] = work[part, :] + in_b[...]
-
-    there = copy(work.at[span(start_b + (1 - bit_c) * size_c, size_c)], in_c, 2, mate_c)
-    there.start()
-    there.wait()
-    part = span(start_c, size_c)
-    work[part, :] = work[part, :] + in_c[...]
-
-    group = []
-    for k in range(1, line):
-        piece = span(start_c + (z + k) % line * size_d, size_d)
-        group.append(copy(work.at[piece], in_d.at[k - 1], 2 + k, mates_d[k - 1]))
-    for there in group:
+    def one(stream):
+        start_a = stream * half + core * size_a
+        start_b = start_a + bit_b * size_b
+        start_c = start_b + bit_c * size_c
+        start_d = start_c + z * size_d
+
+        there = copy(x_ref.at[span(stream * half + (1 - core) * size_a, size_a)], in_a.at[stream], stream * count + 0, mate_a)
         there.start()
-    for there in group:
+        yield
         there.wait()
-    part = span(start_d, size_d)
-    total = work[part, :]
-    for k in range(1, line):
-        total = total + in_d[k - 1]
-    full[part, :] = total
-
-    group = [
-        copy(full.at[part], full.at[part], 1 + line + k, mates_d[k - 1]) for k in range(1, line)
-    ]
-    for there in group:
+        part = span(start_a, size_a)
+        work[part, :] = x_ref[part, :] + in_a[stream]
+
+        there = copy(work.at[span(start_a + (1 - bit_b) * size_b, size_b)], in_b.at[stream], stream * count + 1, mate_b)
         there.start()
-    for there in group:
+        yield
         there.wait()
-    last = 2 * line + 1
-    for number, start, size, mate in (
-        (last, start_c, size_c, mate_c),
-        (last + 1, start_b, size_b, mate_b),
-        (last + 2, start_a, size_a, mate_a),
-    ):
-        part = span(start, size)
-        there = copy(full.at[part], full.at[part], number, mate)
+        part = span(start_b, size_b)
+        work[part, :] = work[part, :] + in_b[stream]
+
+        there = copy(work.at[span(start_b + (1 - bit_c) * size_c, size_c)], in_c.at[stream], stream * count + 2, mate_c)
         there.start()
+        yield
         there.wait()
+        part = span(start_c, size_c)
+        work[part, :] = work[part, :] + in_c[stream]
+
+        group = []
+        for k in range(1, line):
+            piece = span(start_c + (z + k) % line * size_d, size_d)
+            group.append(copy(work.at[piece], in_d.at[stream, k - 1], stream * count + 2 + k, mates_d[k - 1]))
+        for there in group:
+            there.start()
+        yield
+        for there in group:
+            there.wait()
+        part = span(start_d, size_d)
+        total = work[part, :]
+        for k in range(1, line):
+            total = total + in_d[stream, k - 1]
+        full[part, :] = total
+
+        group = [
+            copy(full.at[part], full.at[part], stream * count + 1 + line + k, mates_d[k - 1]) for k in range(1, line)
+        ]
+        for there in group:
+            there.start()
+        yield
+        for there in group:
+            there.wait()
+        last = stream * count + 2 * line + 1
+        for number, start, size, mate in (
+            (last, start_c, size_c, mate_c),
+            (last + 1, start_b, size_b, mate_b),
+            (last + 2, start_a, size_a, mate_a),
+        ):
+            part = span(start, size)
+            there = copy(full.at[part], full.at[part], number, mate)
+            there.start()
+            yield
+            there.wait()
+
+    first, second = one(0), one(1)
+    next(first)
+    for _ in first:
+        next(second)
+    for _ in second:
+        pass
     back = pltpu.make_async_copy(full, out_ref, own)
     back.start()
     back.wait()
@@ -333,7 +348,7 @@
     ens = lax.axis_size("ens")
     rows, width = flat.shape
     line = ens // 2
-    count = 2 * line + 4
+    count = 2 * (2 * line + 4)
     return pl.pallas_call(
         functools.partial(reduce_kernel, ens),
         out_shape=jax.ShapeDtypeStruct(flat.shape, F32),
@@ -342,10 +357,10 @@
         scratch_shapes=[
             pltpu.VMEM((rows, width), F32),
             pltpu.VMEM((rows, width), F32),
-            pltpu.VMEM((rows // 2, width), F32),
-            pltpu.VMEM((rows // 4, width), F32),
-            pltpu.VMEM((rows // 8, width), F32),
-            pltpu.VMEM((line - 1, rows // 8 // line, width), F32),
+            pltpu.VMEM((2, rows // 4, width), F32),
+            pltpu.VMEM((2, rows // 8, width), F32),
+            pltpu.VMEM((2, rows // 16, width), F32),
+            pltpu.VMEM((2, line - 1, rows // 16 // line, width), F32),
             pltpu.SemaphoreType.DMA((count,)),
             pltpu.SemaphoreType.DMA((count,)),
             pltpu.SemaphoreType.DMA,
@@ -480,7 +495,7 @@
     )
 
     base_tail = 3 * width + width + 2 * ffn + width
-    unit = 8 * lax.axis_size("dp") * lax.axis_size("ens")
+    unit = 16 * lax.axis_size("dp") * lax.axis_size("ens")
     used = base_tail + 8 + levels_n * heads
     flat_rows = (used + unit - 1) // unit * unit
     flat = pl.pallas_call(

time: 177 us -> 163 us (0.921)
  Pallas kernels: 147 us -> 133 us
    pallas_call x1, Pallas kernels: 73 us -> 59.6 us  [total_over_all(): pl.pallas_call(functools.partial(reduce_kernel, ens), out_shape=jax.Shape...]
where the time goes in v2:
time: 163 us
  Pallas kernels  133 us (82%)
  local copies, waits for them, and re-layouts  21.6 us (13%)
  other arithmetic  5.89 us (4%)
    pallas_call x1, Pallas kernels, total_over_all(): pl.pallas_call(functools.partial(reduce_kernel, ens), out_shape=jax.Shape...  59.6 us
    pallas_call x1, Pallas kernels, shards(): pl.pallas_call(backward_kernel, grid=(steps,), in_specs=[smem, row_block(...  40.4 us
    pallas_call x1, Pallas kernels, shards(): pl.pallas_call(forward_kernel, grid=(steps,), in_specs=[smem, smem, row_b...  23.1 us
    unnamed x52, local copies, waits for them, and re-layouts  13.8 us
    pallas_call x1, Pallas kernels, total_over_ens(): pl.pallas_call(functools.partial(small_kernel, ens), out_shape=jax.ShapeD...  10.2 us

profile of v2, /device:TPU:0, one launch (start us, length us, event | category | flops | bytes accessed | tf_op | source)
XLA Modules:
  0.0 162.7 jit_solution(5929636062596807348)
XLA Ops:
  0.6 0.0 copy-start
  0.7 0.0 copy-start.24
  0.7 0.0 copy-start.23
  0.7 0.0 copy-start.19
  0.7 0.0 copy-start.17
  0.7 0.0 copy-start.21
  0.7 0.0 copy-start.25
  0.7 0.7 bitcast_convert_fusion
  1.5 0.8 convert_reduce_fusion
  2.2 0.1 pad.11.clone
  2.3 0.1 broadcast_in_dim.16
  2.4 1.2 copy-done.3
  3.6 1.0 copy-done.6
  4.7 1.0 copy-done.8
  5.7 1.0 copy-done.10
  6.7 0.9 copy-done.13
  7.6 0.7 copy-done.15
  8.3 0.7 copy-done.16
  9.0 0.7 copy-done.18
  9.6 0.7 copy-done.20
  10.3 23.1 %forward.1 = (bf16[2048,768]{1,0:T(8,128)(2,1)}, bf16[16,128,1024]{2,1,0:T(8,128)(2,1)}, bf16[2048,256]{1,0:T(8,128)(2,1)S(1)}, f32[2048,256]{1,0:T(8,128)}, f32[8,2,256]{2,1,0:T(2,128)S(1)}) custom-call(s32[16]{0:T(128)S(1)} %bitcast.62, f32[8,8]{1,0:T(8,128)S(1)} %bitcast.61, bf16[2048,256]{1,0:T(8,128)(2,1)S(1)} %bitcast.49, s32[16,128,128]{2,1,0:T(8,128)} %bitcast.51, ...), custom_call_target="tpu_custom_call" | custom-call | tf_op jit(solution)/shard_map/forward/pallas_call | solution.py:444
  33.4 1.0 copy-done.12
  34.4 0.2 fusion.36
  34.6 0.0 copy-done.25
  34.6 0.1 fusion.9
  34.7 0.6 select_maximum_fusion.x_ref
  35.3 10.2 %small.1 = f32[8,384]{1,0:T(8,128)} custom-call(f32[8,384]{1,0:T(8,128)} %select_maximum_fusion.x_ref), custom_call_target="tpu_custom_call" | custom-call | tf_op jit(solution)/shard_map/small/pallas_call | solution.py:401
  45.6 0.8 slice_reduce_fusion.1
  46.4 0.9 multiply_reduce_fusion.3
  47.3 0.5 bitcast_add_fusion
  47.8 0.2 fusion.8
  48.1 0.1 multiply_reduce_fusion.1
  48.2 0.2 fusion.2
  48.4 0.3 fusion
  48.7 0.1 maximum_maximum_fusion.tail_ref
  48.9 0.0 copy-start.11
  48.9 1.0 copy-done.11
  49.9 40.4 %backward.1.x_ref = f32[3584,256]{1,0:T(8,128)} custom-call(s32[16]{0:T(128)S(1)} %bitcast.63, bf16[2048,256]{1,0:T(8,128)(2,1)S(1)} %bitcast.50, s32[16,128,128]{2,1,0:T(8,128)S(1)} %bitcast.52, bf16[2048,768]{1,0:T(8,128)(2,1)} %get-tuple-element.17.proj_ref, bf16[16,128,1024]{2,1,0:T(8,128)(2,1)} %get-tuple-element.18.att_ref, ...), custom_call_target="tpu_custom_call" | custom-call | tf_op jit(solution)/shard_map/backward/pallas_call | solution.py:501
  90.2 2.0 %copy-done.1 = f32[3584,256]{1,0:T(8,128)S(1)} copy-done((f32[3584,256]{1,0:T(8,128)S(1)}, f32[3584,256]{1,0:T(8,128)}, u32[]{:S(2)}) %copy-start.1) | copy-done | bytes 3670040
  92.3 59.6 %reduce.3 = f32[3584,256]{1,0:T(8,128)S(1)} custom-call(f32[3584,256]{1,0:T(8,128)S(1)} %copy-done.1), custom_call_target="tpu_custom_call" | custom-call | tf_op jit(solution)/shard_map/reduce/pallas_call | solution.py:352
  151.9 1.8 %copy-done.2 = f32[3584,256]{1,0:T(8,128)} copy-done((f32[3584,256]{1,0:T(8,128)}, f32[3584,256]{1,0:T(8,128)S(1)}, u32[]{:S(2)}) %copy-start.2) | copy-done | bytes 3670040
  153.7 0.1 slice_reduce_fusion
  153.8 0.7 reshape.81
  154.5 1.4 fusion.37
  155.9 2.3 %slice_bitcast_fusion = f32[1,1024,256]{2,1,0:T(8,128)} fusion(f32[3584,256]{1,0:T(8,128)} %copy-done.2), kind=kLoop, calls=%fused_computation.6 | loop fusion | bytes 2097152 | tf_op jit(solution)/shard_map/broadcast_in_dim | solution.py:537
  158.1 2.5 %fusion.38 = (f32[256,256]{1,0:T(8,128)}, f32[256,256]{1,0:T(8,128)S(1)}, f32[256,256]{1,0:T(8,128)S(1)}, f32[256,256]{1,0:T(8,128)S(1)}, f32[256,256]{1,0:T(8,1...) fusion(f32[3584,256]{1,0:T(8,128)} %copy-done.2), kind=kLoop, calls=%fused_computation.69 | loop fusion | bytes 4718592 | tf_op jit(solution)/shard_map/slice | solution.py:526
  160.7 0.9 maximum_bitcast_fusion.1
  161.6 1.1 maximum_bitcast_fusion
  (35 shorter events, 0.1 us)
Async XLA Ops:
  0.6 33.7 %copy-start = (bf16[256,256]{1,0:T(8,128)(2,1)S(1)}, bf16[256,256]{1,0:T(8,128)(2,1)}, u32[]{:S(2)}) copy-start(bf16[256,256]{1,0:T(8,128)(2,1)} %param.27) | copy-start | bytes 393220
  0.7 45.7 %copy-start.24 = (f32[256]{0:T(256)S(1)}, f32[256]{0:T(256)}, u32[]{:S(2)}) copy-start(f32[256]{0:T(256)} %param.29) | copy-start | bytes 3076
  0.7 45.7 %copy-start.23 = (f32[256]{0:T(256)S(1)}, f32[256]{0:T(256)}, u32[]{:S(2)}) copy-start(f32[256]{0:T(256)} %param.28) | copy-start | bytes 3076
  0.7 48.1 %copy-start.19 = (f32[1,256]{1,0:T(1,128)S(1)}, f32[1,256]{1,0:T(1,128)}, u32[]{:S(2)}) copy-start(f32[1,256]{1,0:T(1,128)} %g2.3) | copy-start | bytes 3076
  0.7 48.1 %copy-start.17 = (f32[1,256]{1,0:T(1,128)S(1)}, f32[1,256]{1,0:T(1,128)}, u32[]{:S(2)}) copy-start(f32[1,256]{1,0:T(1,128)} %g1.3) | copy-start | bytes 3076
  0.7 46.6 %copy-start.22 = (f32[1,4]{1,0:T(1,128)S(1)}, f32[1,4]{1,0:T(1,128)}, u32[]{:S(2)}) copy-start(f32[1,4]{1,0:T(1,128)} %param.19) | copy-start | bytes 52
  0.7 48.1 %copy-start.21 = (s32[1,16]{1,0:T(1,128)S(1)}, s32[1,16]{1,0:T(1,128)}, u32[]{:S(2)}) copy-start(s32[1,16]{1,0:T(1,128)} %param.16) | copy-start | bytes 196
  0.7 33.8 %copy-start.25 = (s32[1,16]{1,0:T(1,128)S(1)}, s32[1,16]{1,0:T(1,128)}, u32[]{:S(2)}) copy-start(s32[1,16]{1,0:T(1,128)} %param.17) | copy-start | bytes 196
  2.4 1.2 copy-start.3
  3.6 1.0 copy-start.6
  4.6 1.0 copy-start.8
  5.7 1.0 copy-start.10
  6.7 0.9 copy-start.13
  7.6 0.7 copy-start.15
  8.3 0.7 copy-start.16
  9.0 0.7 copy-start.18
  9.6 0.7 copy-start.20
  10.3 38.5 %copy-start.4 = (bf16[1,16,128,256]{3,2,1,0:T(8,128)(2,1)S(1)}, bf16[1,16,128,256]{3,2,1,0:T(8,128)(2,1)}, u32[]{:S(2)}) copy-start(bf16[1,16,128,256]{3,2,1,0:T(8,128)(2,1)} %param.15) | copy-start | bytes 3145732
  10.3 38.5 %copy-start.5 = (s32[1,16,128,128]{3,2,1,0:T(8,128)S(1)}, s32[1,16,128,128]{3,2,1,0:T(8,128)}, u32[]{:S(2)}) copy-start(s32[1,16,128,128]{3,2,1,0:T(8,128)} %param.18) | copy-start | bytes 3145732
  10.3 38.5 %copy-start.7 = (bf16[1,256,1024]{2,1,0:T(8,128)(2,1)S(1)}, bf16[1,256,1024]{2,1,0:T(8,128)(2,1)}, u32[]{:S(2)}) copy-start(bf16[1,256,1024]{2,1,0:T(8,128)(2,1)} %param.25) | copy-start | bytes 1572868
  10.3 38.6 %copy-start.9 = (bf16[1,1024,256]{2,1,0:T(8,128)(2,1)S(1)}, bf16[1,1024,256]{2,1,0:T(8,128)(2,1)}, u32[]{:S(2)}) copy-start(bf16[1,1024,256]{2,1,0:T(8,128)(2,1)} %param.26) | copy-start | bytes 1572868
  10.3 38.6 %copy-start.14 = (bf16[1,256,256]{2,1,0:T(8,128)(2,1)S(1)}, bf16[1,256,256]{2,1,0:T(8,128)(2,1)}, u32[]{:S(2)}) copy-start(bf16[1,256,256]{2,1,0:T(8,128)(2,1)} %param.22) | copy-start | bytes 393220
  33.4 1.0 copy-start.12
  48.9 1.0 copy-start.11
  90.2 2.0 %copy-start.1 = (f32[3584,256]{1,0:T(8,128)S(1)}, f32[3584,256]{1,0:T(8,128)}, u32[]{:S(2)}) copy-start(f32[3584,256]{1,0:T(8,128)} %backward.1.x_ref) | copy-start | bytes 11010052
  151.9 1.8 %copy-start.2 = (f32[3584,256]{1,0:T(8,128)}, f32[3584,256]{1,0:T(8,128)S(1)}, u32[]{:S(2)}) copy-start(f32[3584,256]{1,0:T(8,128)S(1)} %reduce.3) | copy-start | bytes 11010052
